TPU v7x, 1024 devices: a whole 4x4x32 slice. The times are simulated.
1024 devices in a mesh: grp: 16 (over x, y), ep: 64 (over z, core).
Axes of the slice: x: 4, y: 4, z: 32, core: 2. Of those that a mesh axis runs over, the one named last changes fastest.
Arguments:
- input_rows: bfloat16 [1024, 256, 2048], P(('grp', 'ep')), may hold values from -6 to 6
- cotangent_rows: bfloat16 [1024, 256, 2048], P(('grp', 'ep')), may hold values from -6 to 6
- gate_probs: float32 [1024, 256], P(('grp', 'ep')), may hold values from 0.05 to 0.5
- row_token: int32 [1024, 256], P(('grp', 'ep')), may hold values from -1 to 1023, as said below
- owner_slot: int32 [16384], P(('grp', 'ep')), may hold values from 0 to 255, as said below
- gate_proj: bfloat16 [64, 2048, 512], P('ep'), may hold values from -0.125 to 0.125
- up_proj: bfloat16 [64, 2048, 512], P('ep'), may hold values from -0.125 to 0.125
- down_proj: bfloat16 [64, 512, 2048], P('ep'), may hold values from -0.25 to 0.25
Outputs:
- input_grad: bfloat16 [16384, 2048], P(('grp', 'ep'))
- prob_grad: float32 [1024, 256], P(('grp', 'ep'))
Inputs may be any that keep to these rules, and one draw needn't show every extreme that they name: `row_token`: within each expert the live rows come first, in increasing token order, then -1. Each token of a group is named by exactly 10 different experts of that group. No expert has more than 4 rows naming tokens of one ep index, and in every group one expert has exactly 4 for every ep index. `owner_slot`: value 16 * owner group + position in the owner's block; the owner lies at the same ep index. Over the tokens of one ep index it is a permutation, and every device processes exactly 1 token of each owner group.
All inputs are finite; a program needn't handle non-finite values.
Results may differ from a plain program's by a relative error of at most 0.0057.
Values may be sent and summed in bfloat16 or wider, within the bound.
A program may use at most 64 MiB of HBM per device.

v0:
```python
import jax
import jax.numpy as jnp
from jax import lax
from jax.sharding import PartitionSpec as P


def expert_backward(inputs, cotangent, probs, gate_w, up_w, down_w):
    wide = jnp.float32
    gate_pre = jnp.einsum("erd,edf->erf", inputs, gate_w, preferred_element_type=wide)
    up_pre = jnp.einsum("erd,edf->erf", inputs, up_w, preferred_element_type=wide)
    grad_act = jnp.einsum("erd,efd->erf", cotangent, down_w, preferred_element_type=wide)
    sigmoid_gate = jax.nn.sigmoid(gate_pre)
    activated = gate_pre * sigmoid_gate
    prob_grad = jnp.sum(grad_act * activated * up_pre, axis=2)
    scaled = probs[:, :, None] * grad_act
    grad_gate = (scaled * up_pre * sigmoid_gate * (1.0 + gate_pre * (1.0 - sigmoid_gate))).astype(
        jnp.bfloat16
    )
    grad_up = (scaled * activated).astype(jnp.bfloat16)
    rows_grad = jnp.einsum("erf,edf->erd", grad_gate, gate_w, preferred_element_type=wide)
    rows_grad = rows_grad + jnp.einsum("erf,edf->erd", grad_up, up_w, preferred_element_type=wide)
    return (rows_grad.astype(jnp.bfloat16), prob_grad)


def on_device(
    input_rows, cotangent_rows, gate_probs, row_token, owner_slot, gate_proj, up_proj, down_proj
):
    rows_grad, prob_grad = expert_backward(
        input_rows, cotangent_rows, gate_probs, gate_proj, up_proj, down_proj
    )
    prob_grad = jnp.where(row_token >= 0, prob_grad, 0.0)
    local_experts, expert_rows, width = input_rows.shape
    tok_dev = owner_slot.shape[0]
    flat_rows = rows_grad.reshape(local_experts * expert_rows, width)
    flat_tokens = row_token.reshape(-1)
    wanted = jnp.arange(lax.axis_size("ep") * tok_dev, dtype=jnp.int32)
    select = (wanted[:, None] == flat_tokens[None, :]).astype(jnp.bfloat16)
    summed = lax.psum_scatter(
        jnp.dot(select, flat_rows, preferred_element_type=jnp.float32),
        "ep",
        scatter_dimension=0,
        tiled=True,
    )
    token_grad = summed.astype(jnp.bfloat16)
    grp_size = lax.axis_size("grp")
    per_group = tok_dev // grp_size
    owner_group = owner_slot // tok_dev
    order = jnp.arange(tok_dev, dtype=jnp.int32)
    same = (owner_group[:, None] == owner_group[None, :]) & (order[None, :] < order[:, None])
    position = jnp.sum(same.astype(jnp.int32), axis=1)
    send_index = owner_group * per_group + position
    send_grad = jnp.zeros((tok_dev, width), jnp.bfloat16).at[send_index].set(token_grad)
    send_pos = jnp.zeros((tok_dev,), jnp.int32).at[send_index].set(owner_slot % tok_dev)
    recv_grad, recv_pos = (
        lax.all_to_all(
            send_grad.reshape(grp_size, per_group, width),
            "grp",
            split_axis=0,
            concat_axis=0,
            tiled=True,
        ),
        lax.all_to_all(
            send_pos.reshape(grp_size, per_group), "grp", split_axis=0, concat_axis=0, tiled=True
        ),
    )
    select = (order[:, None] == recv_pos.reshape(-1)[None, :]).astype(jnp.bfloat16)
    input_grad = jnp.dot(
        select, recv_grad.reshape(tok_dev, width), preferred_element_type=jnp.float32
    )
    return (input_grad.astype(jnp.bfloat16), prob_grad)


def solution(mesh):
    placed = (
        P(("grp", "ep"), None, None),
        P(("grp", "ep"), None, None),
        P(("grp", "ep"), None),
        P(("grp", "ep"), None),
        P(("grp", "ep")),
        P("ep", None, None),
        P("ep", None, None),
        P("ep", None, None),
    )
    return jax.shard_map(
        on_device,
        mesh=mesh,
        in_specs=placed,
        out_specs=(P(("grp", "ep"), None), P(("grp", "ep"), None)),
        check_vma=False,
    )
```

profile of v0, /device:TPU:1, one launch (start us, length us, event | category | flops | bytes accessed | tf_op | source)
XLA Modules:
  0.0 273.9 jit_solution(16276000987989041479)
XLA Ops:
  7.2 0.0 copy-start
  7.2 0.0 reduce-scatter.2.cloned.1.call-start
  7.2 0.0 copy-start.4
  7.2 0.0 copy-start.5
  7.2 2.8 %fusion.3 = f32[256,512]{1,0:T(8,128)S(1)} fusion(bf16[1,2048,512]{2,1,0:T(8,128)(2,1)} %param.13, bf16[1,256,2048]{2,1,0:T(8,128)(2,1)} %param.8), kind=kOutput, calls=%fused_computation.7 | convolution fusion | flops 536870912 | bytes 3670016 | tf_op jit(solution)/shard_map/erd,edf->erf/dot_general | solution.py:9
  10.0 0.0 copy-done.4
  10.0 0.1 copy-done.5
  10.2 0.0 copy-start.6
  10.2 0.7 fusion.8
  10.9 0.0 copy-done
  10.9 0.6 copy-done.6
  11.5 0.0 copy-start.1
  11.5 0.0 copy-start.2
  11.5 0.8 multiply_reduce_fusion
  12.3 0.8 copy-done.1
  13.1 0.0 copy-done.2
  13.1 0.0 copy-start.3
  13.1 2.3 fusion.1
  15.4 0.0 copy-done.3
  15.4 6.7 %fusion.11 = f32[1024,2048]{1,0:T(8,128)} fusion(f32[256,2048]{1,0:T(8,128)} %fusion.1, bf16[1,2048,512]{2,1,0:T(8,128)(2,1)S(1)} %copy-done, s32[256]{0:T(256)S(1)} %bitcast.38, f32[256,512]{1,0:T(8,128)S(1)} %fusion.8, f32[256]{0:T(256)S(1)} %bitcast.37, f32[256,512]{1,0:T(8,128)S(1)} %fusion.3), kind=kOutput, calls=%fused_computation.14 | convolution fusion | flops 1612840960 | bytes 13633536 | tf_op jit(solution)/shard_map/dot_general | solution.py:39
  22.1 0.0 copy-start.7
  22.1 0.0 reduce-scatter.2.cloned.1.call-update
  22.1 0.6 copy-done.7
  22.7 0.2 convert_reduce_fusion
  22.9 0.6 scatter_custom_fusion
  23.6 0.7 copy.13
  24.2 7.6 %all-to-all-start = ((s32[16,1,1]{2,1,0:T(1,128)}), s32[16,1,1]{2,1,0:T(1,128)S(1)}, u32[]{:S(2)}, u32[]{:S(2)}) async-start(s32[16,1,1]{2,1,0:T(1,128)} %copy.13), calls=%async_computation | async-start | bytes 16384 | tf_op jit(solution)/shard_map/all_to_all | solution.py:62
  31.8 218.5 %reduce-scatter.2.cloned.1.call-done = f32[16,2048]{1,0:T(8,128)} async-done(((f32[1024,2048]{1,0:T(8,128)}), f32[16,2048]{1,0:T(8,128)}) %reduce-scatter.2.cloned.1.call-update) | async-done | bytes 131088 | tf_op jit(solution)/shard_map/reduce_scatter | solution.py:38
  250.3 1.1 scatter_custom_fusion.1
  251.4 0.5 broadcast.57
  251.9 0.7 reduce.3
  252.6 0.7 reshape.100
  253.3 0.0 all-to-all-done
  253.3 6.4 %all-to-all-start.1 = ((bf16[16,2,1024]{2,1,0:T(2,128)(2,1)}), bf16[16,2,1024]{2,1,0:T(2,128)(2,1)S(1)}, u32[]{:S(2)}, u32[]{:S(2)}) async-start(bf16[16,2,1024]{2,1,0:T(2,128)(2,1)} %reshape.100), calls=%async_computation.2 | async-start | bytes 131072 | tf_op jit(solution)/shard_map/all_to_all | solution.py:55
  259.7 0.6 compare_select_fusion
  260.2 0.4 reduce.2
  260.6 5.6 %all-to-all-done.1 = bf16[16,2,1024]{2,1,0:T(2,128)(2,1)S(1)} async-done(((bf16[16,2,1024]{2,1,0:T(2,128)(2,1)}), bf16[16,2,1024]{2,1,0:T(2,128)(2,1)S(1)}, u32[]{:S(2)}, u32[]{:S(2)}) %all-to-all-start.1) | async-done | bytes 65568 | tf_op jit(solution)/shard_map/all_to_all | solution.py:55
  266.2 0.1 reshape.101
  266.2 0.8 convolution_convert_fusion
  (2 shorter events, 0.0 us)
Async XLA Ops:
  7.2 3.8 %copy-start = (bf16[1,2048,512]{2,1,0:T(8,128)(2,1)S(1)}, bf16[1,2048,512]{2,1,0:T(8,128)(2,1)}, u32[]{:S(2)}) copy-start(bf16[1,2048,512]{2,1,0:T(8,128)(2,1)} %param.14) | copy-start | bytes 6291460
  7.2 243.1 %reduce-scatter.2.cloned.1.call-start = ((), (), s32[]{:S(2)}) async-start(), calls=%async_computation.3 | async-start | bytes 8519680 | tf_op jit(solution)/shard_map/reduce_scatter | solution.py:38
  7.2 2.8 %copy-start.4 = (bf16[1,512,2048]{2,1,0:T(8,128)(2,1)S(1)}, bf16[1,512,2048]{2,1,0:T(8,128)(2,1)}, u32[]{:S(2)}) copy-start(bf16[1,512,2048]{2,1,0:T(8,128)(2,1)} %param.15) | copy-start | bytes 6291460
  7.2 2.9 %copy-start.5 = (bf16[1,256,2048]{2,1,0:T(8,128)(2,1)S(1)}, bf16[1,256,2048]{2,1,0:T(8,128)(2,1)}, u32[]{:S(2)}) copy-start(bf16[1,256,2048]{2,1,0:T(8,128)(2,1)} %param.9) | copy-start | bytes 3145732
  10.2 1.3 copy-start.6
  11.5 1.6 copy-start.1
  11.5 1.6 copy-start.2
  13.1 2.3 copy-start.3
  22.1 0.7 copy-start.7
  24.2 229.0 %all-to-all-start = ((s32[16,1,1]{2,1,0:T(1,128)}), s32[16,1,1]{2,1,0:T(1,128)S(1)}, u32[]{:S(2)}, u32[]{:S(2)}) async-start(s32[16,1,1]{2,1,0:T(1,128)} %copy.13), calls=%async_computation | async-start | bytes 16384 | tf_op jit(solution)/shard_map/all_to_all | solution.py:62
  253.3 12.9 %all-to-all-start.1 = ((bf16[16,2,1024]{2,1,0:T(2,128)(2,1)}), bf16[16,2,1024]{2,1,0:T(2,128)(2,1)S(1)}, u32[]{:S(2)}, u32[]{:S(2)}) async-start(bf16[16,2,1024]{2,1,0:T(2,128)(2,1)} %reshape.100), calls=%async_computation.2 | async-start | bytes 131072 | tf_op jit(solution)/shard_map/all_to_all | solution.py:55
Sparse Core Ops, SparseCore 0:
  22.2 228.0 reduce-scatter.1
where the time goes:
time: 277 us; the launch traced here: 274 us
  waiting for transfers between devices  224 us (81%)
  matrix products  14.1 us (5%)
  between operations  14.1 us (5%)
  starting transfers between devices  14 us (5%)
  local copies, waits for them, and re-layouts  4.68 us (2%)
  other arithmetic  2.88 us (1%)
    reduce_scatter x1, waiting for transfers between devices, on_device(): lax.psum_scatter(jnp.dot(select, flat_rows, preferred_element_type=jnp.fl...  218 us
    all_to_all x1, starting transfers between devices, on_device(): lax.all_to_all(send_pos.reshape(grp_size, per_group), 'grp', split_axis=0...  7.59 us
    dot_general x1, matrix products, on_device(): jnp.dot(select, flat_rows, preferred_element_type=jnp.float32)  6.7 us
    all_to_all x1, starting transfers between devices, on_device(): lax.all_to_all(send_grad.reshape(grp_size, per_group, width), 'grp', spli...  6.41 us
    all_to_all x1, waiting for transfers between devices, on_device(): lax.all_to_all(send_grad.reshape(grp_size, per_group, width), 'grp', spli...  5.58 us
  transfers between devices with their start and end apart: 3, of which 2 were waited for; matrix products, arithmetic and copies ran while one was open for 2% of the time, Pallas kernels for 0%

commit v1 on v0

v1 whole, which is shorter than its diff:
```python
import functools

import jax
import jax.numpy as jnp
from jax import lax
from jax.experimental import pallas as pl
from jax.experimental.pallas import tpu as pltpu
from jax.sharding import PartitionSpec as P

MESH = pl.DeviceIdType.MESH
WIDE = jnp.float32
HALF = jnp.bfloat16
CHUNKS = 4
K_PARTS = 4
F_PARTS = 2


def nt(a, b):
    return lax.dot_general(a, b, (((1,), (1,)), ((), ())), preferred_element_type=WIDE)


def tn(a, b):
    return lax.dot_general(a, b, (((0,), (0,)), ((), ())), preferred_element_type=WIDE)


def nn(a, b):
    return jnp.dot(a, b, preferred_element_type=WIDE)


def iota(shape, axis):
    return lax.broadcasted_iota(jnp.int32, shape, axis)


def kernel(
    n_grp,
    n_ep,
    x_hbm,
    ct_hbm,
    probs_ref,
    tok_ref,
    own_ref,
    wg_hbm,
    wu_hbm,
    wd_hbm,
    out_ref,
    prob_ref,
    x_ref,
    ct_ref,
    wg_ref,
    wu_ref,
    wd_ref,
    gate_ref,
    up_ref,
    grad_ref,
    sorted_ref,
    rows_ref,
    give_ref,
    part_ref,
    ring_ref,
    note_send,
    note_recv,
    own_send,
    own_recv,
    wide_ref,
    back_send,
    back_recv,
    load_sem,
    note_sems,
    row_send_sem,
    row_recv_sem,
    ring_send_sem,
    ring_recv_sem,
    own_send_sem,
    own_recv_sem,
    back_send_sem,
    back_recv_sem,
):
    rows, width = x_ref.shape
    units = wg_ref.shape[1]
    tok_dev = out_ref.shape[0]
    shift = tok_dev.bit_length() - 1
    n_z = n_ep // 2
    half = n_z // 2
    side = rows // 2
    cw = width // CHUNKS
    lanes = 128
    blocks = width // lanes

    g = lax.axis_index("grp")
    e = lax.axis_index("ep")
    z = e // 2
    core = e % 2
    sibling = 2 * z + (1 - core)
    right = 2 * ((z + 1) % n_z) + core
    left = 2 * ((z + n_z - 1) % n_z) + core

    barrier = pltpu.get_barrier_semaphore()
    for peer in (sibling, right, left):
        pl.semaphore_signal(barrier, inc=1, device_id=(g, peer), device_id_type=MESH)
    for j in range(1, n_grp):
        pl.semaphore_signal(
            barrier, inc=1, device_id=((g + j) % n_grp, e), device_id_type=MESH
        )

    loads = []

    def load(src, dst):
        copy = pltpu.make_async_copy(src, dst, load_sem.at[len(loads)])
        copy.start()
        loads.append(copy)
        return copy

    load_x = load(x_hbm, x_ref)
    k_step = width // K_PARTS
    load_g = [
        load(wg_hbm.at[pl.ds(i * k_step, k_step)], wg_ref.at[pl.ds(i * k_step, k_step)])
        for i in range(K_PARTS)
    ]
    load_u = [
        load(wu_hbm.at[pl.ds(i * k_step, k_step)], wu_ref.at[pl.ds(i * k_step, k_step)])
        for i in range(K_PARTS)
    ]
    load_c = load(ct_hbm, ct_ref)
    f_step = units // F_PARTS
    load_d = [
        load(wd_hbm.at[pl.ds(i * f_step, f_step)], wd_ref.at[pl.ds(i * f_step, f_step)])
        for i in range(F_PARTS)
    ]

    tok = tok_ref[...]
    live = tok >= 0
    column = lax.shift_right_logical(jnp.where(live, tok, 0), shift)
    mine = live & ((column & 1) == core)
    other = live & ((column & 1) != core)
    line = iota((8, rows), 0)
    flags = jnp.where(
        line == 0, mine.astype(WIDE), jnp.where(line == 1, other.astype(WIDE), 0.0)
    ).astype(HALF)
    before = (iota((rows, rows), 0) < iota((rows, rows), 1)).astype(WIDE).astype(HALF)
    rank = nn(flags, before).astype(jnp.int32)
    slot = jnp.where(mine, rank[0:1], jnp.where(other, side + rank[1:2], -1))
    order = (iota((rows, rows), 0) == slot).astype(WIDE).astype(HALF)
    coded = jnp.where(
        line == 0,
        lax.shift_right_logical(column, 1).astype(WIDE),
        jnp.where(
            line == 1,
            (tok & (tok_dev - 1)).astype(WIDE),
            jnp.where(line == 2, live.astype(WIDE), 0.0),
        ),
    ).astype(HALF)
    moved = nt(coded, order)
    place = jnp.where(moved[2:3] > 0.5, moved[0:1] * tok_dev + moved[1:2], -1.0)
    place = place.astype(jnp.int32)
    note_send[...] = jnp.broadcast_to(place[:, side:], note_send.shape)
    own_send[...] = jnp.full(own_send.shape, -1, jnp.int32)
    own_send[:, 0:tok_dev] = jnp.broadcast_to(own_ref[...], (8, tok_dev))

    load_x.wait()
    for i in range(K_PARTS):
        at = pl.ds(i * k_step, k_step)
        load_g[i].wait()
        term = nn(x_ref[:, at], wg_ref[at, :])
        gate_ref[...] = term if i == 0 else gate_ref[...] + term

    pl.semaphore_wait(barrier, 3 + n_grp - 1)

    def note_copy():
        return pltpu.make_async_remote_copy(
            src_ref=note_send,
            dst_ref=note_recv,
            send_sem=note_sems.at[0],
            recv_sem=note_sems.at[1],
            device_id=(g, sibling),
            device_id_type=MESH,
        )

    def own_copy(j):
        return pltpu.make_async_remote_copy(
            src_ref=own_send,
            dst_ref=own_recv.at[pl.ds(pl.multiple_of(g * 8, 8), 8)],
            send_sem=own_send_sem.at[j],
            recv_sem=own_recv_sem.at[j],
            device_id=((g + j) % n_grp, e),
            device_id_type=MESH,
        )

    def own_copy_in(j):
        source = (g + n_grp - j) % n_grp
        return pltpu.make_async_remote_copy(
            src_ref=own_send,
            dst_ref=own_recv.at[pl.ds(pl.multiple_of(source * 8, 8), 8)],
            send_sem=own_send_sem.at[j],
            recv_sem=own_recv_sem.at[j],
            device_id=((g + j) % n_grp, e),
            device_id_type=MESH,
        )

    note_copy().start()
    for j in range(1, n_grp):
        own_copy(j).start()
    own_recv[pl.ds(pl.multiple_of(g * 8, 8), 8), :] = own_send[...]

    for i in range(K_PARTS):
        at = pl.ds(i * k_step, k_step)
        load_u[i].wait()
        term = nn(x_ref[:, at], wu_ref[at, :])
        up_ref[...] = term if i == 0 else up_ref[...] + term

    probs = jnp.transpose(jnp.broadcast_to(probs_ref[...], (lanes, rows)))[:, 0:1]
    load_c.wait()
    prob_sum = jnp.zeros((rows, lanes), WIDE)
    for i in range(F_PARTS):
        at = pl.ds(i * f_step, f_step)
        load_d[i].wait()
        grad_act = nt(ct_ref[...], wd_ref[at, :])
        gate_pre, up_pre = gate_ref[:, at], up_ref[:, at]
        sig = 1.0 / (1.0 + jnp.exp(-gate_pre))
        act = gate_pre * sig
        terms = grad_act * act * up_pre
        for j in range(f_step // lanes):
            prob_sum = prob_sum + terms[:, j * lanes : (j + 1) * lanes]
        scaled = probs * grad_act
        grad_ref[:, i * f_step : (i + 1) * f_step] = (
            scaled * up_pre * sig * (1.0 + gate_pre * (1.0 - sig))
        ).astype(HALF)
        grad_ref[:, units + i * f_step : units + (i + 1) * f_step] = (
            scaled * act
        ).astype(HALF)
    sorted_ref[...] = nn(order, grad_ref[...]).astype(HALF)

    def row_copy(c):
        return pltpu.make_async_remote_copy(
            src_ref=give_ref.at[c],
            dst_ref=rows_ref.at[c, pl.ds(side, side)],
            send_sem=row_send_sem.at[c],
            recv_sem=row_recv_sem.at[c],
            device_id=(g, sibling),
            device_id_type=MESH,
        )

    def make_rows(c):
        at = pl.ds(c * cw, cw)
        made = nt(sorted_ref[:, 0:units], wg_ref[at, :])
        made = (made + nt(sorted_ref[:, units:], wu_ref[at, :])).astype(HALF)
        give_ref[c] = made[side:]
        row_copy(c).start()
        rows_ref[c, 0:side] = made[:side]

    def ring_copy(way, c, s):
        return pltpu.make_async_remote_copy(
            src_ref=ring_ref.at[way, c, s],
            dst_ref=ring_ref.at[way, c, s + 1],
            send_sem=ring_send_sem.at[way, c, s],
            recv_sem=ring_recv_sem.at[way, c, s],
            device_id=(g, right if way == 0 else left),
            device_id_type=MESH,
        )

    def target(way, s):
        away = half - s
        return (z + away) % n_z if way == 0 else (z + n_z - away) % n_z

    def first(way, c):
        return (way + c) % 2

    def ring_start(c):
        for way in range(2):
            s = first(way, c)
            ring_ref[way, c, s] = part_ref[c, target(way, s)].astype(HALF)
            ring_copy(way, c, s).start()

    def ring_step(way, c, s):
        ring_copy(way, c, s - 1).wait_recv()
        total = ring_ref[way, c, s].astype(WIDE) + part_ref[c, target(way, s)]
        ring_ref[way, c, s] = total.astype(HALF)
        ring_copy(way, c, s).start()

    pick = None

    def make_part(c):
        row_copy(c).wait_recv()
        part_ref[c] = nn(pick, rows_ref[c]).reshape(n_z, tok_dev, cw)

    make_rows(0)
    note_copy().wait_recv()
    where_to = jnp.concatenate([place[:, :side], note_recv[0:1, :]], axis=1)
    pick = (iota((n_z * tok_dev, rows), 0) == where_to).astype(WIDE).astype(HALF)
    for c in range(1, CHUNKS):
        make_rows(c)
        make_part(c - 1)
        ring_start(c - 1)
    make_part(CHUNKS - 1)
    ring_start(CHUNKS - 1)

    prob_line = jnp.sum(jnp.transpose(prob_sum), axis=0, keepdims=True)
    prob_ref[...] = jnp.where(live, prob_line, 0.0)

    def one_step(t, carry):
        for c in range(CHUNKS):
            for way in range(2):
                ring_step(way, c, t + first(way, c))
        return carry

    lax.fori_loop(1, half - 1, one_step, 0)
    for c in range(CHUNKS):
        for way in range(2):
            if first(way, c) == 0:
                ring_step(way, c, half - 1)

    group_of = lax.shift_right_logical(own_ref[...], shift)
    to_group = (iota((n_grp, tok_dev), 0) == group_of).astype(WIDE).astype(HALF)
    for c in range(CHUNKS):
        total = part_ref[c, z]
        for way in range(2):
            ring_copy(way, c, half - 1).wait_recv()
            total = total + ring_ref[way, c, half].astype(WIDE)
        lined = nn(to_group, total.astype(HALF))
        for j in range(cw // lanes):
            wide_ref[pl.ds(c * (cw // lanes) + j, n_grp, stride=blocks), :] = lined[
                :, j * lanes : (j + 1) * lanes
            ]
    back_send[...] = wide_ref[...].astype(HALF)

    def back_copy(j, to, into):
        return pltpu.make_async_remote_copy(
            src_ref=back_send.at[pl.ds(pl.multiple_of(to * blocks, blocks), blocks)],
            dst_ref=back_recv.at[pl.ds(pl.multiple_of(into * blocks, blocks), blocks)],
            send_sem=back_send_sem.at[j],
            recv_sem=back_recv_sem.at[j],
            device_id=(to, e),
            device_id_type=MESH,
        )

    for j in range(1, n_grp):
        back_copy(j, (g + j) % n_grp, g).start()
    self_at = pl.ds(pl.multiple_of(g * blocks, blocks), blocks)
    back_recv[self_at, :] = back_send[self_at, :]

    for j in range(1, n_grp):
        own_copy_in(j).wait_recv()
    owners = own_recv[pl.ds(0, n_grp, stride=8), :]
    here = lax.shift_right_logical(owners, shift) == g
    position = jnp.sum(
        jnp.where(here, owners & (tok_dev - 1), 0), axis=1, keepdims=True
    )
    to_place = (iota((n_grp, tok_dev), 1) == position).astype(WIDE).astype(HALF)
    note_copy().wait_send()
    for c in range(CHUNKS):
        row_copy(c).wait_send()
    for j in range(1, n_grp):
        own_copy(j).wait_send()

    def drain(t, carry):
        for c in range(CHUNKS):
            for way in range(2):
                ring_copy(way, c, t + first(way, c)).wait_send()
        return carry

    lax.fori_loop(0, half - 1, drain, 0)
    for c in range(CHUNKS):
        for way in range(2):
            if first(way, c) == 0:
                ring_copy(way, c, half - 1).wait_send()

    for j in range(1, n_grp):
        back_copy(j, (g + j) % n_grp, (g + n_grp - j) % n_grp).wait_recv()
    wide_ref[...] = back_recv[...].astype(WIDE)
    for j in range(blocks):
        block = wide_ref[pl.ds(j, n_grp, stride=blocks), :].astype(HALF)
        out_ref[:, j * lanes : (j + 1) * lanes] = tn(to_place, block).astype(HALF)
    for j in range(1, n_grp):
        back_copy(j, (g + j) % n_grp, g).wait_send()


def on_device(n_grp, n_ep, x, ct, probs, tok, own, wg, wu, wd):
    rows, width = x.shape[1:]
    units = wg.shape[2]
    tok_dev = own.shape[0]
    n_z = n_ep // 2
    half = n_z // 2
    cw = width // CHUNKS
    blocks = width // 128
    anywhere = pl.BlockSpec(memory_space=pl.ANY)
    near = pl.BlockSpec(memory_space=pltpu.VMEM)
    dma = pltpu.SemaphoreType.DMA
    return pl.pallas_call(
        functools.partial(kernel, n_grp, n_ep),
        out_shape=(
            jax.ShapeDtypeStruct((tok_dev, width), HALF),
            jax.ShapeDtypeStruct((1, rows), WIDE),
        ),
        in_specs=[anywhere, anywhere, near, near, near, anywhere, anywhere, anywhere],
        out_specs=(near, near),
        scratch_shapes=[
            pltpu.VMEM((rows, width), HALF),
            pltpu.VMEM((rows, width), HALF),
            pltpu.VMEM((width, units), HALF),
            pltpu.VMEM((width, units), HALF),
            pltpu.VMEM((units, width), HALF),
            pltpu.VMEM((rows, units), WIDE),
            pltpu.VMEM((rows, units), WIDE),
            pltpu.VMEM((rows, 2 * units), HALF),
            pltpu.VMEM((rows, 2 * units), HALF),
            pltpu.VMEM((CHUNKS, rows, cw), HALF),
            pltpu.VMEM((CHUNKS, rows // 2, cw), HALF),
            pltpu.VMEM((CHUNKS, n_z, tok_dev, cw), WIDE),
            pltpu.VMEM((2, CHUNKS, half + 1, tok_dev, cw), HALF),
            pltpu.VMEM((8, rows // 2), jnp.int32),
            pltpu.VMEM((8, rows // 2), jnp.int32),
            pltpu.VMEM((8, 128), jnp.int32),
            pltpu.VMEM((8 * n_grp, 128), jnp.int32),
            pltpu.VMEM((n_grp * blocks, 128), WIDE),
            pltpu.VMEM((n_grp * blocks, 128), HALF),
            pltpu.VMEM((n_grp * blocks, 128), HALF),
            dma((2 + 2 * K_PARTS + F_PARTS,)),
            dma((2,)),
            dma((CHUNKS,)),
            dma((CHUNKS,)),
            dma((2, CHUNKS, half)),
            dma((2, CHUNKS, half)),
            dma((n_grp,)),
            dma((n_grp,)),
            dma((n_grp,)),
            dma((n_grp,)),
        ],
        compiler_params=pltpu.CompilerParams(
            collective_id=0, has_side_effects=True, vmem_limit_bytes=56 * 1024 * 1024
        ),
        cost_estimate=pl.CostEstimate(
            flops=12 * rows * width * units,
            bytes_accessed=2 * (2 * rows * width + 3 * width * units),
            transcendentals=rows * units,
        ),
        name="expert_backward",
    )(
        x.reshape(rows, width),
        ct.reshape(rows, width),
        probs,
        tok,
        own.reshape(1, tok_dev),
        wg.reshape(width, units),
        wu.reshape(width, units),
        wd.reshape(units, width),
    )


def solution(mesh):
    sizes = dict(mesh.shape)
    placed = (
        P(("grp", "ep"), None, None),
        P(("grp", "ep"), None, None),
        P(("grp", "ep"), None),
        P(("grp", "ep"), None),
        P(("grp", "ep")),
        P("ep", None, None),
        P("ep", None, None),
        P("ep", None, None),
    )
    return jax.shard_map(
        functools.partial(on_device, sizes["grp"], sizes["ep"]),
        mesh=mesh,
        in_specs=placed,
        out_specs=(P(("grp", "ep"), None), P(("grp", "ep"), None)),
        check_vma=False,
    )
```

time: 277 us -> 88.8 us (0.32)
  the two profiles are of different devices: /device:TPU:1 before, /device:TPU:32 now
where the time goes in v1:
time: 88.8 us; the launch traced here: 88.6 us
  Pallas kernels  85.3 us (96%)
  local copies, waits for them, and re-layouts  2.67 us (3%)
    pallas_call x1, Pallas kernels, on_device(): pl.pallas_call(functools.partial(kernel, n_grp, n_ep), out_shape=(jax.Sha...  85.3 us
    unnamed x2, local copies, waits for them, and re-layouts  2.67 us

profile of v1, /device:TPU:32, one launch (start us, length us, event | category | flops | bytes accessed | tf_op | source)
XLA Modules:
  0.0 88.6 jit_solution(11729546789054317967)
XLA Ops:
  0.6 85.3 %expert_backward.1 = (bf16[16,2048]{1,0:T(8,128)(2,1)}, f32[1,256]{1,0:T(1,128)}) custom-call(bf16[256,2048]{1,0:T(8,128)(2,1)} %bitcast.9, bf16[256,2048]{1,0:T(8,128)(2,1)} %bitcast.10, f32[1,256]{1,0:T(1,128)} %probs_ref.1, s32[1,256]{1,0:T(1,128)} %tok_ref.1, s32[1,16]{1,0:T(1,128)} %bitcast.11, bf16[2048,512]{1,0:T(8,128)(2,1)} %bitcast.6, ...), custom_call_target="tpu_custom_call" | custom-call | flops 3221225472 | bytes 8388608 | tf_op jit(solution)/shard_map/expert_backward/pallas_call | solution.py:387
  85.9 1.5 %copy.12 = bf16[16,2048]{1,0:T(8,128)(2,1)} copy(bf16[16,2048]{1,0:T(8,128)(2,1)} %get-tuple-element.4) | data formatting | bytes 131072
  87.4 1.2 %copy.13 = f32[1,256]{1,0:T(1,128)} copy(f32[1,256]{1,0:T(1,128)} %get-tuple-element.5) | data formatting | bytes 2048

commit v2 on v1

v2 whole, which is shorter than its diff:
```python
import functools

import jax
import jax.numpy as jnp
from jax import lax
from jax.experimental import pallas as pl
from jax.experimental.pallas import tpu as pltpu
from jax.sharding import PartitionSpec as P

MESH = pl.DeviceIdType.MESH
WIDE = jnp.float32
HALF = jnp.bfloat16
CHUNKS = 4
K_PARTS = 4
F_PARTS = 2


def nt(a, b):
    return lax.dot_general(a, b, (((1,), (1,)), ((), ())), preferred_element_type=WIDE)


def tn(a, b):
    return lax.dot_general(a, b, (((0,), (0,)), ((), ())), preferred_element_type=WIDE)


def nn(a, b):
    return jnp.dot(a, b, preferred_element_type=WIDE)


def iota(shape, axis):
    return lax.broadcasted_iota(jnp.int32, shape, axis)


def kernel(
    n_grp,
    n_ep,
    x_hbm,
    ct_hbm,
    probs_ref,
    tok_ref,
    own_ref,
    wg_hbm,
    wu_hbm,
    wd_hbm,
    out_ref,
    prob_ref,
    x_ref,
    ct_ref,
    wg_ref,
    wu_ref,
    wd_ref,
    gate_ref,
    up_ref,
    grad_ref,
    sorted_ref,
    made_ref,
    rows_ref,
    part_ref,
    ring_ref,
    note_send,
    note_recv,
    own_send,
    own_recv,
    wide_ref,
    back_send,
    back_recv,
    load_sem,
    note_send_sem,
    note_recv_sem,
    row_send_sem,
    row_recv_sem,
    ring_send_sem,
    ring_recv_sem,
    own_send_sem,
    own_recv_sem,
    back_send_sem,
    back_recv_sem,
):
    rows, width = x_ref.shape
    units = wg_ref.shape[1]
    tok_dev = out_ref.shape[0]
    shift = tok_dev.bit_length() - 1
    n_z = n_ep // 2
    half = n_z // 2
    steps = half // 2
    side = rows // 2
    block = side // 4
    cap = block // steps
    turns = steps // 2
    piece = block // 2
    part = 4 * piece
    cw = width // CHUNKS
    lanes = 128
    blocks = width // lanes

    g = lax.axis_index("grp")
    e = lax.axis_index("ep")
    z = e // 2
    core = e % 2

    def chip(away, flip=0):
        at = core if flip == 0 else 1 - core
        return 2 * ((z + n_z + away) % n_z) + at

    near = [chip(0, 1), chip(1), chip(1, 1), chip(-1), chip(-1, 1)]
    far = [chip(2, 1), chip(-2, 1)]
    barrier = pltpu.get_barrier_semaphore()
    for peer in near + far:
        pl.semaphore_signal(barrier, inc=1, device_id=(g, peer), device_id_type=MESH)
    for j in range(1, n_grp):
        pl.semaphore_signal(
            barrier, inc=1, device_id=((g + j) % n_grp, e), device_id_type=MESH
        )

    loads = []

    def load(src, dst):
        copy = pltpu.make_async_copy(src, dst, load_sem.at[len(loads)])
        copy.start()
        loads.append(copy)
        return copy

    load_x = load(x_hbm, x_ref)
    k_step = width // K_PARTS
    load_g = [
        load(wg_hbm.at[pl.ds(i * k_step, k_step)], wg_ref.at[pl.ds(i * k_step, k_step)])
        for i in range(K_PARTS)
    ]
    load_u = [
        load(wu_hbm.at[pl.ds(i * k_step, k_step)], wu_ref.at[pl.ds(i * k_step, k_step)])
        for i in range(K_PARTS)
    ]
    load_c = load(ct_hbm, ct_ref)
    f_step = units // F_PARTS
    load_d = [
        load(wd_hbm.at[pl.ds(i * f_step, f_step)], wd_ref.at[pl.ds(i * f_step, f_step)])
        for i in range(F_PARTS)
    ]

    tok = tok_ref[...]
    live = tok >= 0
    column = lax.shift_right_logical(jnp.where(live, tok, 0), shift)
    away = lax.shift_right_logical(column, 1) - z
    away = jnp.where(away < 0, away + n_z, away)
    odd = away & 1
    up = (away <= half) & (away > 0)
    dist = jnp.where(away <= half, away, n_z - away)
    turn = lax.shift_right_logical(half - odd - dist, 1)
    turn = jnp.where(away == 0, 0, turn)
    kind = jnp.where(up, jnp.where(odd == 1, 1, 0), jnp.where(odd == 1, 2, 3))
    flips = jnp.where(away == 0, 0, (steps - turn) & 1)
    earlier = iota((rows, rows), 0) < iota((rows, rows), 1)
    keyed = jnp.where(live, column, -1).astype(WIDE)
    down_keyed = jnp.transpose(jnp.broadcast_to(keyed, (lanes, rows)))[:, 0:1]
    rank = jnp.sum(
        jnp.where(earlier & (down_keyed == keyed), 1.0, 0.0), axis=0, keepdims=True
    ).astype(jnp.int32)
    late = jnp.where(turn >= turns, 1, 0)
    slot = late * part + kind * piece + (turn - late * turns) * cap + rank
    slot = jnp.where(((column + flips) & 1) == core, slot, slot + side)
    slot = jnp.where(live, slot, -1)
    order = (iota((rows, rows), 0) == slot).astype(WIDE).astype(HALF)
    line = iota((8, rows), 0)
    coded = jnp.where(
        line == 0,
        (tok & (tok_dev - 1)).astype(WIDE),
        jnp.where(
            line == 1,
            (live & (away > 0)).astype(WIDE),
            jnp.where(line == 2, (live & (away == 0)).astype(WIDE), 0.0),
        ),
    ).astype(HALF)
    moved = nt(coded, order)
    at_slot = iota((1, rows), 1) & (part - 1)
    kind_of = lax.shift_right_logical(at_slot, piece.bit_length() - 1)
    turn_of = lax.shift_right_logical(at_slot & (piece - 1), cap.bit_length() - 1)
    token = moved[0:1].astype(jnp.int32)
    chained = turn_of * tok_dev + token + jnp.where(kind_of >= 2, turns * tok_dev, 0)
    chained = jnp.where(moved[1:2] > 0.5, chained, -1)
    odd_kind = (kind_of == 1) | (kind_of == 2)
    kept = jnp.where(odd_kind, chained, -1)
    kept = jnp.where(moved[2:3] > 0.5, 2 * turns * tok_dev + token, kept)
    moved_on = jnp.where(odd_kind, -1, chained)
    note = jnp.where(
        iota((8, rows), 0) == 0,
        jnp.broadcast_to(kept, (8, rows)),
        jnp.broadcast_to(moved_on, (8, rows)),
    )
    note_send[0] = note[:, :side]
    note_send[1] = note[:, side:]
    own_send[...] = jnp.full(own_send.shape, -1, jnp.int32)
    own_send[:, 0:tok_dev] = jnp.broadcast_to(own_ref[...], (8, tok_dev))

    load_x.wait()
    for i in range(K_PARTS):
        at = pl.ds(i * k_step, k_step)
        load_g[i].wait()
        term = nn(x_ref[:, at], wg_ref[at, :])
        gate_ref[...] = term if i == 0 else gate_ref[...] + term
    for i in range(K_PARTS):
        at = pl.ds(i * k_step, k_step)
        load_u[i].wait()
        term = nn(x_ref[:, at], wu_ref[at, :])
        up_ref[...] = term if i == 0 else up_ref[...] + term

    pl.semaphore_wait(barrier, len(near) + len(far) + n_grp - 1)

    def note_copy(i):
        return pltpu.make_async_remote_copy(
            src_ref=note_send.at[0 if i in (1, 3) else 1],
            dst_ref=note_recv.at[i],
            send_sem=note_send_sem.at[i],
            recv_sem=note_recv_sem.at[i],
            device_id=(g, near[i]),
            device_id_type=MESH,
        )

    def own_copy(j, into):
        return pltpu.make_async_remote_copy(
            src_ref=own_send,
            dst_ref=own_recv.at[pl.ds(pl.multiple_of(into * 8, 8), 8)],
            send_sem=own_send_sem.at[j],
            recv_sem=own_recv_sem.at[j],
            device_id=((g + j) % n_grp, e),
            device_id_type=MESH,
        )

    for i in range(len(near)):
        note_copy(i).start()

    probs = jnp.transpose(jnp.broadcast_to(probs_ref[...], (lanes, rows)))[:, 0:1]
    load_c.wait()
    prob_sum = jnp.zeros((rows, lanes), WIDE)
    for i in range(F_PARTS):
        at = pl.ds(i * f_step, f_step)
        load_d[i].wait()
        grad_act = nt(ct_ref[...], wd_ref[at, :])
        gate_pre, up_pre = gate_ref[:, at], up_ref[:, at]
        sig = 1.0 / (1.0 + jnp.exp(-gate_pre))
        act = gate_pre * sig
        terms = grad_act * act * up_pre
        for j in range(f_step // lanes):
            prob_sum = prob_sum + terms[:, j * lanes : (j + 1) * lanes]
        scaled = probs * grad_act
        grad_ref[:, i * f_step : (i + 1) * f_step] = (
            scaled * up_pre * sig * (1.0 + gate_pre * (1.0 - sig))
        ).astype(HALF)
        grad_ref[:, units + i * f_step : units + (i + 1) * f_step] = (
            scaled * act
        ).astype(HALF)
    sorted_ref[...] = nn(order, grad_ref[...]).astype(HALF)

    def row_copy(c, late, i):
        if i == 0:
            count = (2 if late else 3) * piece
            src = made_ref.at[c, pl.ds(side + late * part + piece, count)]
            dst = rows_ref.at[late, c, pl.ds(part + piece, count)]
        else:
            way, flip = (i - 1) // 2, (i - 1) % 2
            at = flip * side + late * part + way * 3 * piece
            src = made_ref.at[c, pl.ds(at, piece)]
            dst = rows_ref.at[late, c, pl.ds(2 * part + (i - 1) * piece, piece)]
        return pltpu.make_async_remote_copy(
            src_ref=src,
            dst_ref=dst,
            send_sem=row_send_sem.at[c, late, i],
            recv_sem=row_recv_sem.at[c, late, i],
            device_id=(g, near[i]),
            device_id_type=MESH,
        )

    def send_rows(c, late):
        for i in (1, 2, 3, 4, 0):
            row_copy(c, late, i).start()

    nothing = jnp.zeros((piece, cw), HALF)

    def make_rows(c):
        at = pl.ds(c * cw, cw)
        made = nt(sorted_ref[:, 0:units], wg_ref[at, :])
        made = (made + nt(sorted_ref[:, units:], wu_ref[at, :])).astype(HALF)
        made_ref[c] = made
        send_rows(c, 0)
        for late in range(2):
            rows_ref[late, c, 0:part] = made[late * part : (late + 1) * part]
            rows_ref[late, c, part : part + piece] = nothing
        rows_ref[1, c, 2 * part - piece : 2 * part] = nothing

    def ring_copy(way, c, s):
        return pltpu.make_async_remote_copy(
            src_ref=ring_ref.at[way, c, s],
            dst_ref=ring_ref.at[way, c, s + 1],
            send_sem=ring_send_sem.at[way, c, s],
            recv_sem=ring_recv_sem.at[way, c, s],
            device_id=(g, near[2 + 2 * way] if s == steps - 1 else far[way]),
            device_id_type=MESH,
        )

    def own_part(way, c, s):
        late = s // turns
        at = (way * turns + s - late * turns) * tok_dev
        return part_ref[late, c, at : at + tok_dev]

    def ring_start(c):
        for way in range(2):
            ring_ref[way, c, 0] = own_part(way, c, 0).astype(HALF)
            ring_copy(way, c, 0).start()

    def ring_step(way, c, s):
        ring_copy(way, c, s - 1).wait_recv()
        total = ring_ref[way, c, s].astype(WIDE) + own_part(way, c, s)
        ring_ref[way, c, s] = total.astype(HALF)
        ring_copy(way, c, s).start()

    for c in range(CHUNKS):
        make_rows(c)
    for i in range(len(near)):
        note_copy(i).wait_recv()
    lane = iota((1, side), 1)

    def rolled(value, by):
        return pltpu.roll(value, by % side, 1) if by % side else value

    def make_pick(late):
        base = late * part
        held = jnp.where(
            lane < part,
            rolled(note_send[0, 0:1], -base),
            rolled(note_recv[0, 0:1], part - base),
        )
        passed = rolled(note_recv[4, 1:2], 3 * piece - base - 3 * piece)
        for q in (2, 1, 0):
            from_at = base + (q // 2) * 3 * piece
            passed = jnp.where(
                lane < (q + 1) * piece,
                rolled(note_recv[1 + q, 1:2], q * piece - from_at),
                passed,
            )
        to = jnp.concatenate([held, passed[:, 0:part]], axis=1)
        count = (2 * turns + 1 - late) * tok_dev
        return (iota((count, 3 * part), 0) == to).astype(WIDE).astype(HALF)

    def make_part(c, late, pick):
        for i in range(5):
            row_copy(c, late, i).wait_recv()
        made = nn(pick, rows_ref[late, c])
        part_ref[late, c, 0 : pick.shape[0]] = made

    pick = make_pick(0)
    for c in range(CHUNKS):
        make_part(c, 0, pick)
        ring_start(c)
    for c in range(CHUNKS):
        send_rows(c, 1)
    pick = make_pick(1)

    prob_line = jnp.sum(jnp.transpose(prob_sum), axis=0, keepdims=True)
    prob_ref[...] = jnp.where(live, prob_line, 0.0)

    own_recv[pl.ds(pl.multiple_of(g * 8, 8), 8), :] = own_send[...]
    to_send = list(range(1, n_grp))
    share = -(-len(to_send) // max(steps - 1, 1))
    for s in range(1, steps):
        if s == min(2, turns):
            for c in range(CHUNKS):
                make_part(c, 1, pick)
        for c in range(CHUNKS):
            for way in range(2):
                ring_step(way, c, s)
        for j in to_send[(s - 1) * share : s * share]:
            own_copy(j, g).start()

    group_of = lax.shift_right_logical(own_ref[...], shift)
    to_group = (iota((n_grp, tok_dev), 0) == group_of).astype(WIDE).astype(HALF)
    for c in range(CHUNKS):
        total = part_ref[0, c, 2 * turns * tok_dev : (2 * turns + 1) * tok_dev]
        for way in range(2):
            ring_copy(way, c, steps - 1).wait_recv()
            total = total + ring_ref[way, c, steps].astype(WIDE)
        lined = nn(to_group, total.astype(HALF))
        for j in range(cw // lanes):
            wide_ref[pl.ds(c * (cw // lanes) + j, n_grp, stride=blocks), :] = lined[
                :, j * lanes : (j + 1) * lanes
            ]
    back_send[...] = wide_ref[...].astype(HALF)

    def back_copy(j, to, into):
        return pltpu.make_async_remote_copy(
            src_ref=back_send.at[pl.ds(pl.multiple_of(to * blocks, blocks), blocks)],
            dst_ref=back_recv.at[pl.ds(pl.multiple_of(into * blocks, blocks), blocks)],
            send_sem=back_send_sem.at[j],
            recv_sem=back_recv_sem.at[j],
            device_id=(to, e),
            device_id_type=MESH,
        )

    for j in range(1, n_grp):
        back_copy(j, (g + j) % n_grp, g).start()
    self_at = pl.ds(pl.multiple_of(g * blocks, blocks), blocks)
    back_recv[self_at, :] = back_send[self_at, :]

    for j in range(1, n_grp):
        own_copy(j, (g + n_grp - j) % n_grp).wait_recv()
    owners = own_recv[pl.ds(0, n_grp, stride=8), :]
    here = lax.shift_right_logical(owners, shift) == g
    position = jnp.sum(
        jnp.where(here, owners & (tok_dev - 1), 0), axis=1, keepdims=True
    )
    to_place = (iota((n_grp, tok_dev), 1) == position).astype(WIDE).astype(HALF)
    for i in range(len(near)):
        note_copy(i).wait_send()
    for c in range(CHUNKS):
        for late in range(2):
            for i in range(5):
                row_copy(c, late, i).wait_send()
    for j in range(1, n_grp):
        own_copy(j, g).wait_send()

    for s in range(steps):
        for c in range(CHUNKS):
            for way in range(2):
                ring_copy(way, c, s).wait_send()

    for j in range(1, n_grp):
        back_copy(j, (g + j) % n_grp, (g + n_grp - j) % n_grp).wait_recv()
    wide_ref[...] = back_recv[...].astype(WIDE)
    for j in range(blocks):
        columns = wide_ref[pl.ds(j, n_grp, stride=blocks), :].astype(HALF)
        out_ref[:, j * lanes : (j + 1) * lanes] = tn(to_place, columns).astype(HALF)
    for j in range(1, n_grp):
        back_copy(j, (g + j) % n_grp, g).wait_send()


def finish(grad_ref, prob_ref, grad_out, prob_out):
    grad_out[...] = grad_ref[...]
    prob_out[...] = prob_ref[...]


def on_device(n_grp, n_ep, x, ct, probs, tok, own, wg, wu, wd):
    rows, width = x.shape[1:]
    units = wg.shape[2]
    tok_dev = own.shape[0]
    steps = n_ep // 8
    cw = width // CHUNKS
    blocks = width // 128
    anywhere = pl.BlockSpec(memory_space=pl.ANY)
    near = pl.BlockSpec(memory_space=pltpu.VMEM)
    dma = pltpu.SemaphoreType.DMA
    results = (
        jax.ShapeDtypeStruct((tok_dev, width), HALF),
        jax.ShapeDtypeStruct((1, rows), WIDE),
    )
    made = pl.pallas_call(
        functools.partial(kernel, n_grp, n_ep),
        out_shape=results,
        in_specs=[anywhere, anywhere, near, near, near, anywhere, anywhere, anywhere],
        out_specs=(near, near),
        scratch_shapes=[
            pltpu.VMEM((rows, width), HALF),
            pltpu.VMEM((rows, width), HALF),
            pltpu.VMEM((width, units), HALF),
            pltpu.VMEM((width, units), HALF),
            pltpu.VMEM((units, width), HALF),
            pltpu.VMEM((rows, units), WIDE),
            pltpu.VMEM((rows, units), WIDE),
            pltpu.VMEM((rows, 2 * units), HALF),
            pltpu.VMEM((rows, 2 * units), HALF),
            pltpu.VMEM((CHUNKS, rows, cw), HALF),
            pltpu.VMEM((2, CHUNKS, 3 * (rows // 4), cw), HALF),
            pltpu.VMEM((2, CHUNKS, (steps + 1) * tok_dev, cw), WIDE),
            pltpu.VMEM((2, CHUNKS, steps + 1, tok_dev, cw), HALF),
            pltpu.VMEM((2, 8, rows // 2), jnp.int32),
            pltpu.VMEM((5, 8, rows // 2), jnp.int32),
            pltpu.VMEM((8, 128), jnp.int32),
            pltpu.VMEM((8 * n_grp, 128), jnp.int32),
            pltpu.VMEM((n_grp * blocks, 128), WIDE),
            pltpu.VMEM((n_grp * blocks, 128), HALF),
            pltpu.VMEM((n_grp * blocks, 128), HALF),
            dma((2 + 2 * K_PARTS + F_PARTS,)),
            dma((5,)),
            dma((5,)),
            dma((CHUNKS, 2, 5)),
            dma((CHUNKS, 2, 5)),
            dma((2, CHUNKS, steps)),
            dma((2, CHUNKS, steps)),
            dma((n_grp,)),
            dma((n_grp,)),
            dma((n_grp,)),
            dma((n_grp,)),
        ],
        compiler_params=pltpu.CompilerParams(
            collective_id=0, has_side_effects=True, vmem_limit_bytes=56 * 1024 * 1024
        ),
        cost_estimate=pl.CostEstimate(
            flops=12 * rows * width * units,
            bytes_accessed=2 * (2 * rows * width + 3 * width * units),
            transcendentals=rows * units,
        ),
        name="expert_backward",
    )(
        x.reshape(rows, width),
        ct.reshape(rows, width),
        probs,
        tok,
        own.reshape(1, tok_dev),
        wg.reshape(width, units),
        wu.reshape(width, units),
        wd.reshape(units, width),
    )
    return pl.pallas_call(
        finish,
        out_shape=results,
        in_specs=[near, near],
        out_specs=(near, near),
        name="results",
    )(*made)


def solution(mesh):
    sizes = dict(mesh.shape)
    placed = (
        P(("grp", "ep"), None, None),
        P(("grp", "ep"), None, None),
        P(("grp", "ep"), None),
        P(("grp", "ep"), None),
        P(("grp", "ep")),
        P("ep", None, None),
        P("ep", None, None),
        P("ep", None, None),
    )
    return jax.shard_map(
        functools.partial(on_device, sizes["grp"], sizes["ep"]),
        mesh=mesh,
        in_specs=placed,
        out_specs=(P(("grp", "ep"), None), P(("grp", "ep"), None)),
        check_vma=False,
    )
```

time: 88.8 us -> 73.3 us (0.83)
  the two profiles are of different devices: /device:TPU:32 before, /device:TPU:1 now
where the time goes in v2:
time: 73.3 us; the launch traced here: 73.1 us
  Pallas kernels  72.5 us (99%)
    pallas_call x1, Pallas kernels, on_device(): pl.pallas_call(functools.partial(kernel, n_grp, n_ep), out_shape=results,...  71 us
    pallas_call x1, Pallas kernels, on_device(): pl.pallas_call(finish, out_shape=results, in_specs=[near, near], out_spec...  1.48 us

profile of v2, /device:TPU:1, one launch (start us, length us, event | category | flops | bytes accessed | tf_op | source)
XLA Modules:
  0.0 73.1 jit_solution(15049515091661827619)
XLA Ops:
  0.6 71.0 %expert_backward.1 = (bf16[16,2048]{1,0:T(8,128)(2,1)}, f32[1,256]{1,0:T(1,128)}) custom-call(bf16[256,2048]{1,0:T(8,128)(2,1)} %bitcast.9, bf16[256,2048]{1,0:T(8,128)(2,1)} %bitcast.10, f32[1,256]{1,0:T(1,128)} %probs_ref.1, s32[1,256]{1,0:T(1,128)} %tok_ref.1, s32[1,16]{1,0:T(1,128)} %bitcast.11, bf16[2048,512]{1,0:T(8,128)(2,1)} %bitcast.6, ...), custom_call_target="tpu_custom_call" | custom-call | flops 3221225472 | bytes 8388608 | tf_op jit(solution)/shard_map/expert_backward/pallas_call | solution.py:453
  71.6 1.5 %results.1 = (bf16[16,2048]{1,0:T(8,128)(2,1)}, f32[1,256]{1,0:T(1,128)}) custom-call(bf16[16,2048]{1,0:T(8,128)(2,1)} %get-tuple-element.4.grad_ref, f32[1,256]{1,0:T(1,128)} %get-tuple-element.5.prob_ref), custom_call_target="tpu_custom_call" | custom-call | tf_op jit(solution)/shard_map/results/pallas_call | solution.py:510

commit v3 on v2

--- a/solution.py
+++ b/solution.py
@@ -36,14 +36,17 @@
     n_ep,
     x_hbm,
     ct_hbm,
-    probs_ref,
-    tok_ref,
-    own_ref,
+    probs_hbm,
+    tok_hbm,
+    own_hbm,
     wg_hbm,
     wu_hbm,
     wd_hbm,
     out_ref,
     prob_ref,
+    probs_ref,
+    tok_ref,
+    own_ref,
     x_ref,
     ct_ref,
     wg_ref,
@@ -104,14 +107,6 @@
 
     near = [chip(0, 1), chip(1), chip(1, 1), chip(-1), chip(-1, 1)]
     far = [chip(2, 1), chip(-2, 1)]
-    barrier = pltpu.get_barrier_semaphore()
-    for peer in near + far:
-        pl.semaphore_signal(barrier, inc=1, device_id=(g, peer), device_id_type=MESH)
-    for j in range(1, n_grp):
-        pl.semaphore_signal(
-            barrier, inc=1, device_id=((g + j) % n_grp, e), device_id_type=MESH
-        )
-
     loads = []
 
     def load(src, dst):
@@ -120,6 +115,9 @@
         loads.append(copy)
         return copy
 
+    load_tok = load(tok_hbm, tok_ref)
+    load_own = load(own_hbm, own_ref)
+    load_probs = load(probs_hbm, probs_ref)
     load_x = load(x_hbm, x_ref)
     k_step = width // K_PARTS
     load_g = [
@@ -137,6 +135,15 @@
         for i in range(F_PARTS)
     ]
 
+    barrier = pltpu.get_barrier_semaphore()
+    for peer in near + far:
+        pl.semaphore_signal(barrier, inc=1, device_id=(g, peer), device_id_type=MESH)
+    for j in range(1, n_grp):
+        pl.semaphore_signal(
+            barrier, inc=1, device_id=((g + j) % n_grp, e), device_id_type=MESH
+        )
+
+    load_tok.wait()
     tok = tok_ref[...]
     live = tok >= 0
     column = lax.shift_right_logical(jnp.where(live, tok, 0), shift)
@@ -188,6 +195,7 @@
     )
     note_send[0] = note[:, :side]
     note_send[1] = note[:, side:]
+    load_own.wait()
     own_send[...] = jnp.full(own_send.shape, -1, jnp.int32)
     own_send[:, 0:tok_dev] = jnp.broadcast_to(own_ref[...], (8, tok_dev))
 
@@ -228,6 +236,7 @@
     for i in range(len(near)):
         note_copy(i).start()
 
+    load_probs.wait()
     probs = jnp.transpose(jnp.broadcast_to(probs_ref[...], (lanes, rows)))[:, 0:1]
     load_c.wait()
     prob_sum = jnp.zeros((rows, lanes), WIDE)
@@ -350,8 +359,6 @@
     for c in range(CHUNKS):
         make_part(c, 0, pick)
         ring_start(c)
-    for c in range(CHUNKS):
-        send_rows(c, 1)
     pick = make_pick(1)
 
     prob_line = jnp.sum(jnp.transpose(prob_sum), axis=0, keepdims=True)
@@ -363,8 +370,10 @@
     for s in range(1, steps):
         if s == min(2, turns):
             for c in range(CHUNKS):
+                send_rows(c, 1)
+        for c in range(CHUNKS):
+            if s == turns:
                 make_part(c, 1, pick)
-        for c in range(CHUNKS):
             for way in range(2):
                 ring_step(way, c, s)
         for j in to_send[(s - 1) * share : s * share]:
@@ -453,9 +462,12 @@
     made = pl.pallas_call(
         functools.partial(kernel, n_grp, n_ep),
         out_shape=results,
-        in_specs=[anywhere, anywhere, near, near, near, anywhere, anywhere, anywhere],
+        in_specs=[anywhere] * 8,
         out_specs=(near, near),
         scratch_shapes=[
+            pltpu.VMEM((1, rows), WIDE),
+            pltpu.VMEM((1, rows), jnp.int32),
+            pltpu.VMEM((1, tok_dev), jnp.int32),
             pltpu.VMEM((rows, width), HALF),
             pltpu.VMEM((rows, width), HALF),
             pltpu.VMEM((width, units), HALF),
@@ -476,7 +488,7 @@
             pltpu.VMEM((n_grp * blocks, 128), WIDE),
             pltpu.VMEM((n_grp * blocks, 128), HALF),
             pltpu.VMEM((n_grp * blocks, 128), HALF),
-            dma((2 + 2 * K_PARTS + F_PARTS,)),
+            dma((5 + 2 * K_PARTS + F_PARTS,)),
             dma((5,)),
             dma((5,)),
             dma((CHUNKS, 2, 5)),

time: 73.3 us -> 71.8 us (0.980)
  Pallas kernels: 72.5 us -> 70.9 us
    pallas_call x1, Pallas kernels: 71 us -> 69.5 us  [on_device(): pl.pallas_call(functools.partial(kernel, n_grp, n_ep), out_shape=results,...]
where the time goes in v3:
time: 71.8 us; the launch traced here: 71.6 us
  Pallas kernels  70.9 us (99%)
    pallas_call x1, Pallas kernels, on_device(): pl.pallas_call(functools.partial(kernel, n_grp, n_ep), out_shape=results,...  69.5 us
    pallas_call x1, Pallas kernels, on_device(): pl.pallas_call(finish, out_shape=results, in_specs=[near, near], out_spec...  1.48 us

profile of v3, /device:TPU:1, one launch (start us, length us, event | category | flops | bytes accessed | tf_op | source)
XLA Modules:
  0.0 71.6 jit_solution(15226401488552512042)
XLA Ops:
  0.6 69.5 %expert_backward.1 = (bf16[16,2048]{1,0:T(8,128)(2,1)}, f32[1,256]{1,0:T(1,128)}) custom-call(bf16[256,2048]{1,0:T(8,128)(2,1)} %bitcast.9, bf16[256,2048]{1,0:T(8,128)(2,1)} %bitcast.10, f32[1,256]{1,0:T(1,128)} %probs_hbm.1, s32[1,256]{1,0:T(1,128)} %tok_hbm.1, s32[1,16]{1,0:T(1,128)} %bitcast.11, bf16[2048,512]{1,0:T(8,128)(2,1)} %bitcast.6, ...), custom_call_target="tpu_custom_call" | custom-call | flops 3221225472 | bytes 8388608 | tf_op jit(solution)/shard_map/expert_backward/pallas_call | solution.py:462
  70.1 1.5 %results.1 = (bf16[16,2048]{1,0:T(8,128)(2,1)}, f32[1,256]{1,0:T(1,128)}) custom-call(bf16[16,2048]{1,0:T(8,128)(2,1)} %get-tuple-element.4.grad_ref, f32[1,256]{1,0:T(1,128)} %get-tuple-element.5.prob_ref), custom_call_target="tpu_custom_call" | custom-call | tf_op jit(solution)/shard_map/results/pallas_call | solution.py:522
